TPU v7x, 512 devices: a whole 4x8x8 slice. The times are simulated.
512 devices in a mesh: ctx: 64 (over x, z, core), head: 8 (over y).
Axes of the slice: x: 4, y: 8, z: 8, core: 2. Of those that a mesh axis runs over, the one named last changes fastest.
Arguments:
- queries: bfloat16 [8192, 1024], P('ctx', 'head'), may hold values from -200 to 200
- keys: bfloat16 [2, 8192, 128], P(None, 'ctx'), may hold values from -8 to 8
- values: bfloat16 [2, 8192, 128], P(None, 'ctx'), may hold values from -6 to 6
- grad_out: bfloat16 [8192, 1024], P('ctx', 'head'), may hold values from -6 to 6
- episode_lengths: int32 [8], replicated, may hold values from 1 to 4096, 8192 in all
- key_stretches: int32 [128, 4], replicated, may hold values from 0 to 127, as said below
Outputs:
- attn_out: bfloat16 [8192, 1024], P('ctx', 'head')
- grad_queries: bfloat16 [8192, 1024], P('ctx', 'head')
- grad_keys: bfloat16 [2, 8192, 128], P(None, 'ctx')
- grad_values: bfloat16 [2, 8192, 128], P(None, 'ctx')
Inputs may be any that keep to these rules, and one draw needn't show every extreme that they name: Row k of key_stretches (device d = k // 2) lists the stretch of row k itself; 2 stretches up to 7 before it, clipped at 0; and one recall entry: the later of the two stretches of device (d + 32) mod (64) that lie before row k's stretch, or row k's own stretch if neither does. Entries may repeat.
All inputs are finite; a program needn't handle non-finite values.
Results may differ from a plain program's by a relative error of at most 0.017.
Values may be sent and summed in bfloat16 or wider, within the bound.
A program may use at most 64 MiB of HBM per device.

v0:
```python
import math

import jax
import jax.numpy as jnp
from jax import lax
from jax.sharding import PartitionSpec as P

QUERY_HEADS = 8
KEY_VALUE_HEADS = 2
C = 64


mask_floor = -1e30


def row_positions(row_ids, stretch_rows, stretch_total):
    array_stretch = row_ids // stretch_rows
    device_row = array_stretch // 2
    global_stretch = jnp.where(array_stretch % 2 == 0, device_row, stretch_total - 1 - device_row)
    return global_stretch * stretch_rows + row_ids % stretch_rows


def episode_of(positions, episode_ends):
    return jnp.sum((episode_ends[None, :] <= positions[:, None]).astype(jnp.int32), axis=1)


def on_device(queries, keys, values, grad_out, episode_lengths, key_stretches):
    stretch_rows = C
    ctx_count = lax.axis_size("ctx")
    stretch_total = 2 * ctx_count
    tok_dev = queries.shape[0]
    head_dim = keys.shape[2]
    per_device = queries.shape[1] // head_dim
    key_value_group = lax.axis_index("head") * per_device // (QUERY_HEADS // KEY_VALUE_HEADS)
    inv_scale = 1.0 / math.sqrt(head_dim)
    ctx_index = lax.axis_index("ctx")
    episode_ends = jnp.cumsum(episode_lengths)
    my_rows = ctx_index * tok_dev + jnp.arange(tok_dev, dtype=jnp.int32)
    my_pos = row_positions(my_rows, stretch_rows, stretch_total)
    my_eps = episode_of(my_pos, episode_ends)
    my_local = jnp.arange(tok_dev, dtype=jnp.int32) // stretch_rows
    stretch_ids = jnp.arange(stretch_total, dtype=jnp.int32)
    my_lists = lax.dynamic_slice_in_dim(key_stretches, ctx_index * 2, 2, 0)
    query_table = jnp.take(
        jnp.any(my_lists[:, :, None] == stretch_ids[None, None, :], axis=1), my_local, axis=0
    )
    my_stretches = jnp.stack([ctx_index, stretch_total - 1 - ctx_index])
    owner_table = jnp.any(key_stretches[:, :, None] == my_stretches[None, None, :], axis=1)
    my_keys = lax.dynamic_index_in_dim(keys, key_value_group, 0, keepdims=False)
    my_values = lax.dynamic_index_in_dim(values, key_value_group, 0, keepdims=False)
    query_heads = queries.reshape(tok_dev, per_device, head_dim)
    grad_heads = grad_out.reshape(tok_dev, per_device, head_dim)

    def key_visible(row_count):
        row_ids = jnp.arange(row_count, dtype=jnp.int32)
        key_pos = row_positions(row_ids, stretch_rows, stretch_total)
        key_eps = episode_of(key_pos, episode_ends)
        listed = jnp.take(
            query_table, jnp.clip(key_pos // stretch_rows, 0, stretch_total - 1), axis=1
        )
        return (
            (key_pos[None, :] <= my_pos[:, None])
            & (key_eps[None, :] == my_eps[:, None])
            & listed
            & True
        )

    blocks_in = (
        lax.all_gather(my_keys, "ctx", axis=0, tiled=True),
        lax.all_gather(my_values, "ctx", axis=0, tiled=True),
    )
    key_block = blocks_in[0]
    run_max = jnp.full((tok_dev, per_device), mask_floor, jnp.float32)
    visible = key_visible(key_block.shape[0])[:, None, :]
    scores = (
        jnp.einsum("qhd,kd->qhk", query_heads, key_block, preferred_element_type=jnp.float32)
        * inv_scale
    )
    masked = jnp.where(visible, scores, mask_floor)
    new_max = jnp.maximum(run_max, jnp.max(masked, axis=2))
    weights = jnp.where(visible, jnp.exp(masked - new_max[:, :, None]), 0.0)
    run_sum = jnp.sum(weights, axis=2)
    added = jnp.einsum(
        "qhk,kd->qhd",
        weights.astype(jnp.bfloat16),
        blocks_in[1],
        preferred_element_type=jnp.float32,
    )
    final_state = (new_max, run_sum, added)
    run_max, run_sum, run_acc = final_state
    log_total = run_max + jnp.log(run_sum)
    output = run_acc / run_sum[:, :, None]
    inner = jnp.sum(grad_heads.astype(jnp.float32) * output, axis=2)
    attn_out = output.reshape(tok_dev, per_device * head_dim).astype(jnp.bfloat16)
    blocks_in = (
        lax.all_gather(my_keys, "ctx", axis=0, tiled=True),
        lax.all_gather(my_values, "ctx", axis=0, tiled=True),
    )
    key_block = blocks_in[0]
    visible = key_visible(key_block.shape[0])[:, None, :]
    scores = (
        jnp.einsum("qhd,kd->qhk", query_heads, key_block, preferred_element_type=jnp.float32)
        * inv_scale
    )
    weights = jnp.where(
        visible, jnp.exp(jnp.where(visible, scores, mask_floor) - log_total[:, :, None]), 0.0
    )
    grad_weights = jnp.einsum(
        "qhd,kd->qhk", grad_heads, blocks_in[1], preferred_element_type=jnp.float32
    )
    grad_scores = (weights * (grad_weights - inner[:, :, None])).astype(jnp.bfloat16)
    query_total = jnp.einsum(
        "qhk,kd->qhd", grad_scores, key_block, preferred_element_type=jnp.float32
    )
    grad_queries = (
        (query_total * inv_scale).reshape(tok_dev, per_device * head_dim).astype(jnp.bfloat16)
    )
    all_totals, all_inner = (
        lax.all_gather(log_total, "ctx", axis=0, tiled=True),
        lax.all_gather(inner, "ctx", axis=0, tiled=True),
    )
    blocks_in = (
        lax.all_gather(queries, "ctx", axis=0, tiled=True),
        lax.all_gather(grad_out, "ctx", axis=0, tiled=True),
    )
    row_count = blocks_in[0].shape[0]
    query_block = blocks_in[0]
    row_count = query_block.shape[0]
    row_ids = jnp.arange(row_count, dtype=jnp.int32)
    query_pos = row_positions(row_ids, stretch_rows, stretch_total)
    query_eps = episode_of(query_pos, episode_ends)
    owner_rows = jnp.take(
        owner_table, jnp.clip(row_ids // stretch_rows, 0, stretch_total - 1), axis=0
    )
    listed = jnp.take(owner_rows, my_local, axis=1)
    visible = (
        (my_pos[None, :] <= query_pos[:, None])
        & (my_eps[None, :] == query_eps[:, None])
        & listed
        & True
    )[:, None, :]
    block_queries = query_block.reshape(row_count, per_device, head_dim)
    block_grads = blocks_in[1].reshape(row_count, per_device, head_dim)
    scores = (
        jnp.einsum("qhd,kd->qhk", block_queries, my_keys, preferred_element_type=jnp.float32)
        * inv_scale
    )
    weights = jnp.where(
        visible, jnp.exp(jnp.where(visible, scores, mask_floor) - all_totals[:, :, None]), 0.0
    )
    value_total = jnp.einsum(
        "qhk,qhd->kd", weights.astype(jnp.bfloat16), block_grads, preferred_element_type=jnp.float32
    )
    grad_weights = jnp.einsum(
        "qhd,kd->qhk", block_grads, my_values, preferred_element_type=jnp.float32
    )
    grad_scores = (weights * (grad_weights - all_inner[:, :, None])).astype(jnp.bfloat16)
    key_total = jnp.einsum(
        "qhk,qhd->kd", grad_scores, block_queries, preferred_element_type=jnp.float32
    )
    key_total, value_total = (key_total, value_total)
    group_slot = (jnp.arange(keys.shape[0], dtype=jnp.int32) == key_value_group)[:, None, None]
    key_part = jnp.where(group_slot, (key_total * inv_scale)[None], 0.0)
    value_part = jnp.where(group_slot, value_total[None], 0.0)
    key_sum, value_sum = (
        lax.psum(key_part.astype(jnp.bfloat16), "head").astype(jnp.float32),
        lax.psum(value_part.astype(jnp.bfloat16), "head").astype(jnp.float32),
    )
    return (attn_out, grad_queries, key_sum.astype(jnp.bfloat16), value_sum.astype(jnp.bfloat16))


def solution(mesh):
    return jax.shard_map(
        on_device,
        mesh=mesh,
        in_specs=(
            P("ctx", "head"),
            P(None, "ctx", None),
            P(None, "ctx", None),
            P("ctx", "head"),
            P(),
            P(),
        ),
        out_specs=(P("ctx", "head"), P("ctx", "head"), P(None, "ctx", None), P(None, "ctx", None)),
        check_vma=False,
    )
```

profile of v0, /device:TPU:1, one launch (start us, length us, event | category | flops | bytes accessed | tf_op | source)
XLA Modules:
  0.0 440.9 jit_solution(12701860682242251586)
XLA Ops:
  7.2 0.8 copy-done
  8.0 0.6 constant_dynamic-slice_fusion.1
  8.7 1.4 constant_dynamic-slice_fusion
  10.2 0.7 all-gather.11.cloned.1.call-update
  10.9 0.5 all-gather.13.cloned.1.call-update
  11.5 0.9 copy.30
  12.5 0.8 compare_reduce_fusion
  13.4 22.9 %gather_fusion.1 = pred[8192,2]{1,0:T(8,128)(4,1)S(1)} fusion(pred[128,2]{1,0:T(8,128)(4,1)S(1)} %copy.31, s32[8192]{0:T(1024)S(1)} %broadcast_clamp_fusion), kind=kCustom, calls=%fused_computation.2 | custom fusion | bytes 65536 | tf_op jit(solution)/shard_map/jit(_take)/gather | solution.py:132
  36.3 4.3 broadcast_select_fusion
  40.9 0.7 gather_fusion
  42.0 1.4 copy.32
  43.3 5.3 %gather_fusion.2 = pred[128,8192]{1,0:T(32,128)(4,1)S(1)} fusion(pred[8192,2]{0,1:T(4,128)(4,1)S(1)} %copy.32, s32[1024]{0:T(1024)S(1)} %pad_clamp_fusion), kind=kCustom, calls=%fused_computation.3 | custom fusion | bytes 2097664 | tf_op jit(solution)/shard_map/jit(_take)/gather | solution.py:135
  48.7 22.9 %gather_fusion.3 = pred[8192,128]{1,0:T(32,128)(4,1)S(1)} fusion(pred[128,128]{0,1:T(8,128)(4,1)S(1)} %copy.29, s32[8192]{0:T(1024)S(1)} %broadcast_clamp_fusion.1), kind=kCustom, calls=%fused_computation.clone | custom fusion | bytes 2129920 | tf_op jit(solution)/shard_map/jit(_take)/gather | solution.py:58
  71.9 29.3 %all-gather.15.cloned.1.call-done = bf16[1,8192,128]{2,1,0:T(8,128)(2,1)} async-done(((bf16[1,128,128]{2,1,0:T(8,128)(2,1)}), bf16[1,8192,128]{2,1,0:T(8,128)(2,1)}) %all-gather.15.cloned.1.call-update) | async-done | bytes 2097168 | tf_op jit(solution)/shard_map/all_gather | solution.py:69
  101.3 8.1 %fusion.73 = (f32[128]{0:T(128)S(1)}, f32[128,8192]{0,1:T(8,128)S(1)}) fusion(bf16[128,128]{1,0:T(8,128)(2,1)S(1)} %copy-done.6, bf16[1,8192,128]{2,1,0:T(8,128)(2,1)} %all-gather.15.cloned.1.call-done, pred[8192,128]{1,0:T(32,128)(4,1)S(1)} %gather_fusion.3, pred[8192]{0:T(1024)(128)(4,1)S(1)} %compare_and_fusion, s32[128]{0:T(128)S(1)} %convert_reduce_fusion.1, ...), kind=kOutput, calls=%fused_computation.133 | convolution fusion | flops 276823936 | bytes 7448064 | tf_op jit(solution)/shard_map/qhd,kd->qhk/dot_general | solution.py:76
  109.3 1.9 copy-done.2
  111.3 6.5 %fusion.13 = f32[128]{0:T(128)S(1)} fusion(f32[128,8192]{0,1:T(8,128)S(1)} %get-tuple-element.28, f32[128]{0:T(128)S(1)} %broadcast_maximum_fusion, pred[8192,128]{1,0:T(32,128)(4,1)S(1)} %gather_fusion.3, pred[8192]{0:T(1024)(128)(4,1)S(1)} %compare_and_fusion, s32[128]{0:T(128)S(1)} %convert_reduce_fusion.1, s32[8192]{0:T(1024)S(1)} %convert_reduce_fusion, ...), kind=kLoop, calls=%fused_computation.24 | loop fusion | flops 8388480 | bytes 5318656 | tf_op jit(solution)/shard_map/reduce_sum | solution.py:82
  117.8 38.1 %all-gather.4 = f32[64,1,128]{2,1,0:T(1,128)S(1)} all-gather(f32[1,1,128]{2,1,0:T(1,128)S(1)} %bitcast.107), channel_id=4, replica_groups=mesh['ctx'=64,'head'=8] {'ctx'}, dimensions={0}, use_global_device_ids=true | all-gather | bytes 33280 | tf_op jit(solution)/shard_map/all_gather | solution.py:119
  155.9 30.0 %all-gather.17.cloned.1.call-done = bf16[1,8192,128]{2,1,0:T(8,128)(2,1)} async-done(((bf16[1,128,128]{2,1,0:T(8,128)(2,1)}), bf16[1,8192,128]{2,1,0:T(8,128)(2,1)}) %all-gather.17.cloned.1.call-update) | async-done | bytes 2097168 | tf_op jit(solution)/shard_map/all_gather | solution.py:70
  185.8 8.2 %multiply_reduce_fusion = (f32[128]{0:T(128)S(1)}, bf16[128,128]{0,1:T(8,128)(2,1)S(1)}) fusion(bf16[128,128]{0,1:T(8,128)(2,1)S(1)} %copy.30, f32[128]{0:T(128)S(1)} %fusion.13, bf16[1,8192,128]{2,1,0:T(8,128)(2,1)} %all-gather.17.cloned.1.call-done, f32[128,8192]{0,1:T(8,128)} %copy-done.2, f32[128]{0:T(128)S(1)} %broadcast_maximum_fusion, ...), kind=kOutput, calls=%fused_computation.52 | convolution fusion | flops 276905856 | bytes 7481856 | tf_op jit(solution)/shard_map/qhk,kd->qhd/dot_general | solution.py:83
  194.0 38.2 %all-gather.5 = f32[64,1,128]{2,1,0:T(1,128)S(1)} all-gather(f32[1,1,128]{2,1,0:T(1,128)S(1)} %bitcast.108), channel_id=5, replica_groups=mesh['ctx'=64,'head'=8] {'ctx'}, dimensions={0}, use_global_device_ids=true | all-gather | bytes 33280 | tf_op jit(solution)/shard_map/all_gather | solution.py:120
  232.3 37.6 %all-gather.11.cloned.1.call-done = bf16[8192,128]{1,0:T(8,128)(2,1)} async-done(((bf16[128,128]{1,0:T(8,128)(2,1)}), bf16[8192,128]{1,0:T(8,128)(2,1)}) %all-gather.11.cloned.1.call-update) | async-done | bytes 2097168 | tf_op jit(solution)/shard_map/all_gather | solution.py:123
  269.8 5.8 %fusion.10 = f32[8192,128]{0,1:T(8,128)} fusion(bf16[8192,128]{1,0:T(8,128)(2,1)} %all-gather.11.cloned.1.call-done, pred[128,8192]{1,0:T(32,128)(4,1)S(1)} %gather_fusion.2, f32[8192]{0:T(1024)S(1)} %bitcast.106, s32[8192]{0:T(1024)S(1)} %convert_reduce_fusion, s32[8192]{0:T(1024)S(1)} %fusion.53, s32[128]{0:T(128)S(1)} %convert_reduce_fusion.1, ...), kind=kOutput, calls=%fused_computation.18 | convolution fusion | flops 277872640 | bytes 7472256 | tf_op jit(solution)/shard_map/qhd,kd->qhk/dot_general | solution.py:145
  275.7 78.0 %all-gather.13.cloned.1.call-done = bf16[8192,128]{1,0:T(8,128)(2,1)} async-done(((bf16[128,128]{1,0:T(8,128)(2,1)}), bf16[8192,128]{1,0:T(8,128)(2,1)}) %all-gather.13.cloned.1.call-update) | async-done | bytes 2097168 | tf_op jit(solution)/shard_map/all_gather | solution.py:124
  353.7 3.7 fusion.22
  357.4 4.1 fusion.29
  361.6 0.7 select_convert_fusion
  362.4 8.3 %fusion.35 = bf16[128,128]{1,0:T(8,128)(2,1)} fusion(bf16[1,8192,128]{2,1,0:T(8,128)(2,1)} %all-gather.15.cloned.1.call-done, bf16[128,128]{1,0:T(8,128)(2,1)S(1)} %copy-done.4, f32[128,8192]{0,1:T(8,128)} %copy-done.2, bf16[1,8192,128]{2,1,0:T(8,128)(2,1)} %all-gather.17.cloned.1.call-done, f32[128]{0:T(128)S(1)} %get-tuple-element.23, ...), kind=kOutput, calls=%fused_computation.40 | convolution fusion | flops 547389440 | bytes 9578496 | tf_op jit(solution)/shard_map/qhk,kd->qhd/dot_general | solution.py:112
  370.7 0.7 copy.33
  371.4 60.0 %all-reduce.3.cloned.1.call-done = (bf16[2,128,128]{2,1,0:T(8,128)(2,1)}, bf16[2,128,128]{2,1,0:T(8,128)(2,1)}) async-done(((bf16[2,128,128]{2,1,0:T(8,128)(2,1)}, bf16[2,128,128]{2,1,0:T(8,128)(2,1)}), (bf16[2,128,128]{2,1,0:T(8,128)(2,1)}, bf16[2,128,128]{2,1,0:T(8,128)(2,1)})) %all-reduce.3.cloned.1.call-update) | async-done | bytes 131088 | tf_op jit(solution)/shard_map/psum | solution.py:166
  431.4 1.5 copy.41
  432.9 1.5 copy.42
  (47 shorter events, 1.6 us)
Async XLA Ops:
  7.2 0.8 copy-start
  7.2 94.1 %all-gather.15.cloned.1.call-start = ((), (), s32[]{:S(2)}) async-start(), calls=%async_computation.2 | async-start | bytes 2129920 | tf_op jit(solution)/shard_map/all_gather | solution.py:69
  8.7 177.2 %all-gather.17.cloned.1.call-start = ((), (), s32[]{:S(2)}) async-start(), calls=%async_computation.3 | async-start | bytes 2129920 | tf_op jit(solution)/shard_map/all_gather | solution.py:70
  10.1 259.7 %all-gather.11.cloned.1.call-start = ((), (), s32[]{:S(2)}) async-start(), calls=%async_computation | async-start | bytes 2129920 | tf_op jit(solution)/shard_map/all_gather | solution.py:123
  10.8 342.9 %all-gather.13.cloned.1.call-start = ((), (), s32[]{:S(2)}) async-start(), calls=%async_computation.1 | async-start | bytes 2129920 | tf_op jit(solution)/shard_map/all_gather | solution.py:124
  11.4 420.0 %all-reduce.3.cloned.1.call-start = ((), (), s32[]{:S(2)}) async-start(), calls=%async_computation.4 | async-start | bytes 262144 | tf_op jit(solution)/shard_map/psum | solution.py:166
  13.4 27.2 %copy-start.7 = (s32[128,4]{0,1:T(4,128)S(1)}, s32[128,4]{0,1:T(4,128)}, u32[]{:S(2)}) copy-start(s32[128,4]{0,1:T(4,128)} %param.13) | copy-start | bytes 6148
  13.4 28.4 %copy-start.8 = (s32[8]{0:T(128)S(1)}, s32[8]{0:T(128)}, u32[]{:S(2)}) copy-start(s32[8]{0:T(128)} %param.12) | copy-start | bytes 100
  48.7 52.6 %copy-start.6 = (bf16[128,128]{1,0:T(8,128)(2,1)S(1)}, bf16[128,128]{1,0:T(8,128)(2,1)}, u32[]{:S(2)}) copy-start(bf16[128,128]{1,0:T(8,128)(2,1)} %param.8) | copy-start | bytes 98308
  109.3 1.9 copy-start.2
  155.9 114.0 %copy-start.5 = (bf16[1,128,128]{2,1,0:T(8,128)(2,1)S(1)}, bf16[1,128,128]{2,1,0:T(8,128)(2,1)}, u32[]{:S(2)}) copy-start(bf16[1,128,128]{2,1,0:T(8,128)(2,1)} %constant_dynamic-slice_fusion.1) | copy-start | bytes 98308
  275.7 81.7 %copy-start.3 = (bf16[1,128,128]{2,1,0:T(8,128)(2,1)S(1)}, bf16[1,128,128]{2,1,0:T(8,128)(2,1)}, u32[]{:S(2)}) copy-start(bf16[1,128,128]{2,1,0:T(8,128)(2,1)} %constant_dynamic-slice_fusion) | copy-start | bytes 98308
  353.7 3.7 copy-start.1
  357.4 4.9 %copy-start.4 = (bf16[128,128]{1,0:T(8,128)(2,1)S(1)}, bf16[128,128]{1,0:T(8,128)(2,1)}, u32[]{:S(2)}) copy-start(bf16[128,128]{1,0:T(8,128)(2,1)} %param.11) | copy-start | bytes 98308
Sparse Core Ops, SparseCore 0:
  11.9 89.2 all-gather.14
  105.2 80.5 all-gather.16
  189.2 80.6 all-gather.10
  273.1 80.6 all-gather.12
  362.5 68.8 all-reduce.2
where the time goes:
time: 446 us; the launch traced here: 441 us
  waiting for transfers between devices  236 us (53%)
  blocking collectives  76.3 us (17%)
  local copies, waits for them, and re-layouts  62.8 us (14%)
  matrix products  38.3 us (9%)
  between operations  14 us (3%)
  other arithmetic  13.2 us (3%)
    all_gather x1, waiting for transfers between devices, on_device(): lax.all_gather(grad_out, 'ctx', axis=0, tiled=True)  78 us
    psum x1, waiting for transfers between devices, on_device(): lax.psum(key_part.astype(jnp.bfloat16), 'head').astype(jnp.float32)  60 us
    all_gather x1, blocking collectives, on_device(): lax.all_gather(inner, 'ctx', axis=0, tiled=True)  38.2 us
    all_gather x1, blocking collectives, on_device(): lax.all_gather(log_total, 'ctx', axis=0, tiled=True)  38.1 us
    all_gather x1, waiting for transfers between devices, on_device(): lax.all_gather(queries, 'ctx', axis=0, tiled=True)  37.6 us
    all_gather x1, waiting for transfers between devices, on_device(): lax.all_gather(my_values, 'ctx', axis=0, tiled=True)  30 us
    all_gather x1, waiting for transfers between devices, on_device(): lax.all_gather(my_keys, 'ctx', axis=0, tiled=True)  29.3 us
    gather x1, local copies, waits for them, and re-layouts, key_visible(): jnp.take(query_table, jnp.clip(key_pos // stretch_rows, 0, stretch_total...  22.9 us
  transfers between devices with their start and end apart: 5, of which 5 were waited for; matrix products, arithmetic and copies ran while one was open for 23% of the time, Pallas kernels for 0%

commit v1 on v0

v1 whole, which is shorter than its diff:
```python
import functools
import math

import jax
import jax.numpy as jnp
from jax import lax
from jax.experimental import pallas as pl
from jax.experimental.pallas import tpu as pltpu
from jax.sharding import PartitionSpec as P

MESH = pl.DeviceIdType.MESH
C = 64
QUARTER = 16
HEADS = 8
GROUP = 4
PAIRS = 64
CHIPS = 32
SLOTS = 11
OWN, OTHER, RECALL = 7, 8, 9
D = 128
MASKED = -1e30
EVEN_STEPS = (1, 2, 3)
ODD_STEPS = (1, 2, 3, 4)
INV = 1.0 / math.sqrt(D)


def device_of(pair):
    pair = lax.rem(pair + 2 * PAIRS, PAIRS)
    return jnp.where(pair < PAIRS // 2, 2 * pair, 2 * PAIRS - 1 - 2 * pair)


def attend_kernel(
    q_hbm, k_hbm, v_hbm, do_hbm, ep_hbm, ks_hbm,
    rows_out, sums_out,
    q_ref, do_ref, kv_ref, bias_ref, part_ref, back_ref, rows_ref, quarter_ref, heads_ref,
    ep_ref, ks_ref,
    in_sems, kv_sem, q_sem, back_sem, rows_sem, heads_sem, sums_sem,
    kv_send, q_send, back_send, rows_send, heads_send, sums_send,
):
    d = lax.axis_index("ctx")
    h = lax.axis_index("head")
    m, c = d // 2, d % 2
    g, j = h // GROUP, h % GROUP
    mine = jnp.where(c == 0, m, PAIRS - 1 - m)
    other = PAIRS - 1 - mine
    other_core = 2 * m + 1 - c
    far_chip = lax.rem(m + CHIPS // 2, CHIPS)
    late = jnp.where(m >= CHIPS // 2, 1, 0)

    even_to = [device_of(mine + k) for k in EVEN_STEPS]
    even_from = [device_of(mine - k) for k in EVEN_STEPS]
    odd_with = [device_of(other + k) for k in ODD_STEPS]
    far = [2 * far_chip, 2 * far_chip + 1]
    heads = [(h + k) % HEADS for k in range(1, HEADS)]
    group_heads = [g * GROUP + (j + k) % GROUP for k in range(1, GROUP)]

    barrier = pltpu.get_barrier_semaphore()

    def greet(ctx_at, head_at):
        pl.semaphore_signal(barrier, inc=1, device_id=(ctx_at, head_at), device_id_type=MESH)

    for at in even_to + even_from + [other_core] + far:
        greet(at, h)
    for at in odd_with:
        pl.when(at != d)(functools.partial(greet, at, h))
    for at in heads:
        greet(d, at)

    even_rows, odd_rows = pl.ds(c * C, C), pl.ds((1 - c) * C, C)
    loads = [
        pltpu.make_async_copy(ep_hbm, ep_ref, in_sems.at[0]),
        pltpu.make_async_copy(ks_hbm, ks_ref, in_sems.at[1]),
    ]
    own_q = [
        pltpu.make_async_copy(q_hbm.at[even_rows], q_ref.at[0], in_sems.at[2]),
        pltpu.make_async_copy(do_hbm.at[even_rows], do_ref.at[0], in_sems.at[3]),
    ]
    own_kv = [
        pltpu.make_async_copy(k_hbm.at[g, even_rows], kv_ref.at[OWN, 0], kv_sem),
        pltpu.make_async_copy(v_hbm.at[g, even_rows], kv_ref.at[OWN, 1], kv_sem),
    ]
    for copy in loads + own_q + own_kv:
        copy.start()

    self_count = jnp.where(lax.rem(mine, PAIRS // 2) < 2, 1, 0)
    pl.semaphore_wait(barrier, 6 + 4 + 1 + 2 + 7 - self_count)

    kv_sends, kv_maybe = [], []

    def send_kv(rows, slot, at, may_be_self=False):
        for which, ref in enumerate((k_hbm, v_hbm)):
            remote = pltpu.make_async_remote_copy(
                src_ref=ref.at[g, rows], dst_ref=kv_ref.at[slot, which], send_sem=kv_send, recv_sem=kv_sem,
                device_id=(at, h), device_id_type=MESH,
            )
            if may_be_self:
                local = pltpu.make_async_copy(ref.at[g, rows], kv_ref.at[slot, which], kv_sem)
                pl.when(at != d)(remote.start)
                pl.when(at == d)(local.start)
                kv_maybe.append((at, remote))
            else:
                remote.start()
                kv_sends.append(remote)

    for k, at in zip(ODD_STEPS[::-1], odd_with[::-1]):
        send_kv(odd_rows, 8 - 2 * k, at, may_be_self=True)
    for k, at in zip(EVEN_STEPS[::-1], even_to[::-1]):
        send_kv(even_rows, 7 - 2 * k, at)
    far_rows = pl.ds(late * C, C)
    for at in far:
        send_kv(far_rows, RECALL + c, at)
    send_kv(odd_rows, OTHER, other_core)
    q_sends = [
        pltpu.make_async_remote_copy(
            src_ref=ref.at[odd_rows], dst_ref=to.at[1], send_sem=q_send.at[n], recv_sem=q_sem.at[n],
            device_id=(other_core, h), device_id_type=MESH,
        )
        for n, (ref, to) in enumerate(((q_hbm, q_ref), (do_hbm, do_ref)))
    ]
    for copy in q_sends:
        copy.start()

    for copy in loads:
        copy.wait()
    lane = lax.broadcasted_iota(jnp.int32, (1, 2 * C), 1)
    query_pos = 2 * mine * C + lane
    first_pos = jnp.zeros_like(query_pos)
    start = jnp.int32(0)
    for e in range(HEADS - 1):
        start = start + ep_ref[e]
        first_pos = jnp.where(start <= query_pos, start, first_pos)
    row_of = (2 * d + c, 2 * other_core + c)
    entries = [[ks_ref[e, row] for e in range(4)] for row in row_of]
    far_valid = jnp.logical_or(late == 1, c == 1)
    key_row = lax.broadcasted_iota(jnp.int32, (C, 2 * C), 0)
    for slot in range(SLOTS):
        if slot < RECALL:
            stretch = 2 * mine - 7 + slot
        else:
            at = far[slot - RECALL]
            stretch = jnp.where(far_valid, jnp.where(late == 1, at, 2 * PAIRS - 1 - at), -1)
        base = []
        for row in entries:
            hit = row[0] == stretch
            for entry in row[1:]:
                hit = jnp.logical_or(hit, entry == stretch)
            base.append(jnp.where(hit, stretch * C, -(1 << 20)))
        key_pos = key_row + jnp.where(lane < C, base[0], base[1])
        seen = (key_pos >= first_pos) & (key_pos <= query_pos)
        bias_ref[pl.ds(slot * C, C), :] = jnp.where(seen, 0.0, MASKED)

    for copy in own_q:
        copy.wait()
    for copy in q_sends:
        copy.wait_recv()
    pltpu.make_async_copy(kv_ref, kv_ref, kv_sem).wait()

    queries = q_ref[...].reshape(2 * C, D)
    grads = do_ref[...].reshape(2 * C, D)
    keys = kv_ref[:, 0].reshape(SLOTS * C, D)
    values = kv_ref[:, 1].reshape(SLOTS * C, D)
    last = (((1,), (1,)), ((), ()))
    first = (((0,), (0,)), ((), ()))
    plain = (((1,), (0,)), ((), ()))

    def dot(a, b, dims):
        return lax.dot_general(a, b, dims, preferred_element_type=jnp.float32)

    scores = dot(keys, queries, last) * INV + bias_ref[...]
    top = jnp.max(scores, axis=0, keepdims=True)
    weights = jnp.exp(scores - top)
    weights = weights * (1.0 / jnp.sum(weights, axis=0, keepdims=True))
    grad_weights = dot(values, grads, last)
    inner = jnp.sum(weights * grad_weights, axis=0, keepdims=True)
    rounded = weights.astype(jnp.bfloat16)
    grad_scores = (weights * (grad_weights - inner)).astype(jnp.bfloat16)
    part_ref[:, 0] = (dot(grad_scores, queries, plain) * INV).astype(jnp.bfloat16).reshape(SLOTS, C, D)
    part_ref[:, 1] = dot(rounded, grads, plain).astype(jnp.bfloat16).reshape(SLOTS, C, D)

    back_sends, back_maybe = [], []

    def send_back(slot, to, at, may_be_self=False):
        remote = pltpu.make_async_remote_copy(
            src_ref=part_ref.at[slot], dst_ref=back_ref.at[to], send_sem=back_send, recv_sem=back_sem,
            device_id=(at, h), device_id_type=MESH,
        )
        if may_be_self:
            local = pltpu.make_async_copy(part_ref.at[slot], back_ref.at[to], back_sem)
            pl.when(at != d)(remote.start)
            pl.when(at == d)(local.start)
            back_maybe.append((at, remote))
        else:
            remote.start()
            back_sends.append(remote)

    for k, at in zip(ODD_STEPS[::-1], odd_with[::-1]):
        send_back(8 - 2 * k, k - 1, at, may_be_self=True)
    for k, at in zip(EVEN_STEPS[::-1], even_from[::-1]):
        send_back(7 - 2 * k, 4 + k, at)
    for n, at in enumerate(far):
        send_back(RECALL + n, 8 + c, at)
    send_back(OTHER, 4, other_core)

    out = dot(rounded, values, first)
    grad_queries = dot(grad_scores, keys, first) * INV
    rows_ref[0] = out.astype(jnp.bfloat16)
    rows_ref[1] = grad_queries.astype(jnp.bfloat16)
    rows_copies = [
        pltpu.make_async_copy(rows_ref.at[n, pl.ds(0, C)], rows_out.at[n, even_rows], in_sems.at[n])
        for n in range(2)
    ]
    rows_sends = [
        pltpu.make_async_remote_copy(
            src_ref=rows_ref.at[n, pl.ds(C, C)], dst_ref=rows_out.at[n, even_rows],
            send_sem=rows_send.at[n], recv_sem=rows_sem.at[n],
            device_id=(other_core, h), device_id_type=MESH,
        )
        for n in range(2)
    ]
    for copy in rows_copies + rows_sends:
        copy.start()

    pltpu.make_async_copy(back_ref, back_ref, back_sem).wait()

    def read(n):
        return back_ref[n].astype(jnp.float32)

    recalled = read(8) + read(9)
    to_even = jnp.where(late == c, 1.0, 0.0)
    even_total = part_ref[OWN].astype(jnp.float32) + read(5) + read(6) + read(7) + recalled * to_even
    odd_total = read(4) + read(0) + read(1) + read(2) + read(3) + recalled * (1.0 - to_even)
    for q in range(GROUP):
        rows = slice(q * QUARTER, (q + 1) * QUARTER)
        quarter_ref[q, c] = even_total[:, rows].astype(jnp.bfloat16)
        quarter_ref[q, 1 - c] = odd_total[:, rows].astype(jnp.bfloat16)
    head_sends = [
        pltpu.make_async_remote_copy(
            src_ref=quarter_ref.at[at % GROUP], dst_ref=heads_ref.at[k], send_sem=heads_send, recv_sem=heads_sem,
            device_id=(d, at), device_id_type=MESH,
        )
        for k, at in enumerate(group_heads)
    ]
    for copy in head_sends:
        copy.start()
    total = quarter_ref[j].astype(jnp.float32)
    pltpu.make_async_copy(heads_ref, heads_ref, heads_sem).wait()
    for k in range(GROUP - 1):
        total = total + heads_ref[k].astype(jnp.float32)
    sums_out[h] = total.astype(jnp.bfloat16)
    sum_sends = [
        pltpu.make_async_remote_copy(
            src_ref=sums_out.at[h], dst_ref=sums_out.at[h], send_sem=sums_send.at[k], recv_sem=sums_sem.at[k],
            device_id=(d, at), device_id_type=MESH,
        )
        for k, at in enumerate(heads)
    ]
    for copy in sum_sends:
        copy.start()

    for copy in rows_copies:
        copy.wait()
    for copy in rows_sends:
        copy.wait_send()
        copy.wait_recv()
    for copy in q_sends + kv_sends + back_sends + head_sends:
        copy.wait_send()
    for at, copy in kv_maybe + back_maybe:
        pl.when(at != d)(copy.wait_send)
    for copy in sum_sends:
        copy.wait_send()
        copy.wait_recv()


def lay_out_kernel(rows_ref, sums_ref, out_ref, dq_ref, dk_ref, dv_ref):
    out_ref[...] = rows_ref[0]
    dq_ref[...] = rows_ref[1]
    for h in range(HEADS):
        g, q = divmod(h, GROUP)
        for s in range(2):
            rows = slice(s * C + q * QUARTER, s * C + (q + 1) * QUARTER)
            dk_ref[g, rows] = sums_ref[h, s, 0]
            dv_ref[g, rows] = sums_ref[h, s, 1]


def on_device(queries, keys, values, grad_out, episode_lengths, key_stretches):
    vmem = pl.BlockSpec(memory_space=pltpu.VMEM)
    dma = pltpu.SemaphoreType.DMA
    bf16 = jnp.bfloat16
    inputs = [
        pltpu.with_memory_space_constraint(x, pltpu.HBM)
        for x in (queries, keys, values, grad_out, episode_lengths, key_stretches.T)
    ]
    rows, sums = pl.pallas_call(
        attend_kernel,
        out_shape=(
            pltpu.VMEM((2, 2 * C, D), bf16),
            pltpu.VMEM((HEADS, 2, 2, QUARTER, D), bf16),
        ),
        in_specs=[pl.BlockSpec(memory_space=pltpu.HBM)] * 6,
        out_specs=(vmem, vmem),
        scratch_shapes=[
            pltpu.VMEM((2, C, D), bf16),
            pltpu.VMEM((2, C, D), bf16),
            pltpu.VMEM((SLOTS, 2, C, D), bf16),
            pltpu.VMEM((SLOTS * C, 2 * C), jnp.float32),
            pltpu.VMEM((SLOTS, 2, C, D), bf16),
            pltpu.VMEM((SLOTS - 1, 2, C, D), bf16),
            pltpu.VMEM((2, 2 * C, D), bf16),
            pltpu.VMEM((GROUP, 2, 2, QUARTER, D), bf16),
            pltpu.VMEM((GROUP - 1, 2, 2, QUARTER, D), bf16),
            pltpu.SMEM((HEADS,), jnp.int32),
            pltpu.SMEM((4, 2 * PAIRS), jnp.int32),
            dma((4,)), dma, dma((2,)), dma, dma((2,)), dma, dma((HEADS - 1,)),
            dma, dma((2,)), dma, dma((2,)), dma, dma((HEADS - 1,)),
        ],
        compiler_params=pltpu.CompilerParams(
            collective_id=0, has_side_effects=True, vmem_limit_bytes=16 * 1024 * 1024
        ),
        name="attend",
    )(*inputs)
    half = jax.ShapeDtypeStruct((2 * C, D), bf16)
    both = jax.ShapeDtypeStruct((2, 2 * C, D), bf16)
    return pl.pallas_call(
        lay_out_kernel,
        out_shape=(half, half, both, both),
        in_specs=[vmem] * 2,
        out_specs=(vmem,) * 4,
        name="lay_out",
    )(*(pltpu.with_memory_space_constraint(x, pltpu.VMEM) for x in (rows, sums)))


def solution(mesh):
    return jax.shard_map(
        on_device,
        mesh=mesh,
        in_specs=(
            P("ctx", "head"),
            P(None, "ctx", None),
            P(None, "ctx", None),
            P("ctx", "head"),
            P(),
            P(),
        ),
        out_specs=(P("ctx", "head"), P("ctx", "head"), P(None, "ctx", None), P(None, "ctx", None)),
        check_vma=False,
    )
```

time: 446 us -> 40.9 us (0.09)
  the two profiles are of different devices: /device:TPU:1 before, /device:TPU:23 now
where the time goes in v1:
time: 40.9 us; the launch traced here: 40.7 us
  Pallas kernels  40.1 us (98%)
  between operations  0.64 us (2%)
    pallas_call x1, Pallas kernels, on_device(): pl.pallas_call(attend_kernel, out_shape=(pltpu.VMEM((2, 2 * C, D), bf16),...  39.4 us

profile of v1, /device:TPU:23, one launch (start us, length us, event | category | flops | bytes accessed | tf_op | source)
XLA Modules:
  0.0 40.7 jit_solution(16957725220999399621)
XLA Ops:
  0.6 39.4 %attend.1 = (bf16[2,128,128]{2,1,0:T(8,128)(2,1)S(1)}, bf16[8,2,2,16,128]{4,3,2,1,0:T(8,128)(2,1)S(1)}) custom-call(bf16[128,128]{1,0:T(8,128)(2,1)} %q_hbm.1, bf16[2,128,128]{2,1,0:T(8,128)(2,1)} %k_hbm.1, bf16[2,128,128]{2,1,0:T(8,128)(2,1)} %v_hbm.1, bf16[128,128]{1,0:T(8,128)(2,1)} %do_hbm.1, s32[8]{0:T(128)} %ep_hbm.1, s32[4,128]{1,0:T(4,128)} %bitcast.1), custom_call_target="tpu_custom_call" | custom-call | tf_op jit(solution)/shard_map/attend/pallas_call | solution.py:293
  40.0 0.7 %lay_out.1 = (bf16[128,128]{1,0:T(8,128)(2,1)}, bf16[128,128]{1,0:T(8,128)(2,1)}, bf16[2,128,128]{2,1,0:T(8,128)(2,1)}, bf16[2,128,128]{2,1,0:T(8,128)(2,1)}) custom-call(bf16[2,128,128]{2,1,0:T(8,128)(2,1)S(1)} %get-tuple-element.6.rows_ref, bf16[8,2,2,16,128]{4,3,2,1,0:T(8,128)(2,1)S(1)} %get-tuple-element.7.sums_ref), custom_call_target="tpu_custom_call" | custom-call | tf_op jit(solution)/shard_map/lay_out/pallas_call | solution.py:323

commit v2 on v1

v2 whole, which is shorter than its diff:
```python
import functools
import math

import jax
import jax.numpy as jnp
from jax import lax
from jax.experimental import pallas as pl
from jax.experimental.pallas import tpu as pltpu
from jax.sharding import PartitionSpec as P

MESH = pl.DeviceIdType.MESH
C = 64
HALF = 32
QUARTER = 16
HEADS = 8
GROUP = 4
PAIR = 2
PAIRS = 64
ROWS = PAIR * 2 * C
CHIPS = 32
SLOTS = 11
OWN, OTHER, RECALL = 7, 8, 9
D = 128
MASKED = -1e30
EVEN_STEPS = (1, 2, 3)
ODD_STEPS = (1, 2, 3, 4)
INV = 1.0 / math.sqrt(D)


def device_of(pair):
    pair = lax.rem(pair + 2 * PAIRS, PAIRS)
    return jnp.where(pair < PAIRS // 2, 2 * pair, 2 * PAIRS - 1 - 2 * pair)


def attend_kernel(
    q_hbm, k_hbm, v_hbm, do_hbm, ep_hbm, ks_hbm,
    rows_out, sums_out,
    qdo_ref, kv_ref, bias_ref, stat_ref, part_ref, back_ref, rows_ref, got_ref,
    ep_ref, ks_ref,
    in_sems, kv_sem, q_sem, stat_sem, back_sem, rows_sem, sums_sem,
    kv_send, q_send, stat_send, back_send, rows_send, sums_send,
):
    d = lax.axis_index("ctx")
    h = lax.axis_index("head")
    m, c = d // 2, d % 2
    g, p, b = h // GROUP, h // PAIR % 2, h % PAIR
    mate = h + 1 - 2 * b
    across = h + 2 - 4 * p
    mine = jnp.where(c == 0, m, PAIRS - 1 - m)
    other = PAIRS - 1 - mine
    other_core = 2 * m + 1 - c
    far_chip = lax.rem(m + CHIPS // 2, CHIPS)
    late = jnp.where(m >= CHIPS // 2, 1, 0)

    even_to = [device_of(mine + k) for k in EVEN_STEPS]
    even_from = [device_of(mine - k) for k in EVEN_STEPS]
    odd_with = [device_of(other + k) for k in ODD_STEPS]
    far = [2 * far_chip, 2 * far_chip + 1]
    heads = [(h + k) % HEADS for k in (4, 3, 5, 2, 6, 1, 7)]

    barrier = pltpu.get_barrier_semaphore()

    def greet(ctx_at, head_at):
        pl.semaphore_signal(barrier, inc=1, device_id=(ctx_at, head_at), device_id_type=MESH)

    for at in odd_with[::-1]:
        pl.when(at != d)(functools.partial(greet, at, h))
        greet(at, across)
    for at in even_to + even_from + far + [other_core]:
        greet(at, h)
        greet(at, across)
    for at in heads:
        greet(d, at)
    greet(other_core, mate)

    even_rows, odd_rows = pl.ds(c * C, C), pl.ds((1 - c) * C, C)
    loads = [
        pltpu.make_async_copy(ep_hbm, ep_ref, in_sems.at[0]),
        pltpu.make_async_copy(ks_hbm, ks_ref, in_sems.at[1]),
    ]
    own = [
        pltpu.make_async_copy(q_hbm.at[even_rows], qdo_ref.at[0, b, 0], q_sem),
        pltpu.make_async_copy(do_hbm.at[even_rows], qdo_ref.at[1, b, 0], q_sem),
        pltpu.make_async_copy(k_hbm.at[g, pl.ds(c * C + b * HALF, HALF)], kv_ref.at[OWN, 0], kv_sem),
        pltpu.make_async_copy(v_hbm.at[g, pl.ds(c * C + b * HALF, HALF)], kv_ref.at[OWN, 1], kv_sem),
    ]
    for copy in loads + own:
        copy.start()

    self_count = jnp.where(lax.rem(mine, PAIRS // 2) < 2, 1, 0)
    pl.semaphore_wait(barrier, 2 * (6 + 4 + 1 + 2) + 7 + 1 - self_count)

    sent, sent_maybe = [], []

    def send_kv(stretch, slot, at, may_be_self=False):
        rows = pl.ds(stretch * C + b * HALF, HALF)
        for which, ref in enumerate((k_hbm, v_hbm)):
            remote = pltpu.make_async_remote_copy(
                src_ref=ref.at[g, rows], dst_ref=kv_ref.at[slot, which], send_sem=kv_send, recv_sem=kv_sem,
                device_id=(at, h), device_id_type=MESH,
            )
            if may_be_self:
                local = pltpu.make_async_copy(ref.at[g, rows], kv_ref.at[slot, which], kv_sem)
                pl.when(at != d)(remote.start)
                pl.when(at == d)(local.start)
                sent_maybe.append((at, remote))
            else:
                remote.start()
                sent.append(remote)

    def send_q(rows, which, to):
        for n, ref in enumerate((q_hbm, do_hbm)):
            remote = pltpu.make_async_remote_copy(
                src_ref=ref.at[rows], dst_ref=qdo_ref.at[n, b, which], send_sem=q_send, recv_sem=q_sem,
                device_id=to, device_id_type=MESH,
            )
            remote.start()
            sent.append(remote)

    for k, at in zip(ODD_STEPS[::-1], odd_with[::-1]):
        send_kv(1 - c, 8 - 2 * k, at, may_be_self=True)
    send_q(even_rows, 0, (d, mate))
    send_q(odd_rows, 1, (other_core, mate))
    for k, at in zip(EVEN_STEPS[::-1], even_to[::-1]):
        send_kv(c, 7 - 2 * k, at)
    for at in far:
        send_kv(late, RECALL + c, at)
    send_kv(1 - c, OTHER, other_core)
    send_q(odd_rows, 1, (other_core, h))

    for copy in loads:
        copy.wait()
    lane = lax.broadcasted_iota(jnp.int32, (1, 2 * C), 1)
    query_pos = 2 * mine * C + lane
    first_pos = jnp.zeros_like(query_pos)
    start = jnp.int32(0)
    for e in range(HEADS - 1):
        start = start + ep_ref[e]
        first_pos = jnp.where(start <= query_pos, start, first_pos)
    row_of = (2 * d + c, 2 * other_core + c)
    entries = [[ks_ref[e, row] for e in range(4)] for row in row_of]
    far_valid = jnp.logical_or(late == 1, c == 1)
    key_row = lax.broadcasted_iota(jnp.int32, (HALF, 2 * C), 0) + b * HALF
    for slot in range(SLOTS):
        if slot < RECALL:
            stretch = 2 * mine - 7 + slot
        else:
            at = far[slot - RECALL]
            stretch = jnp.where(far_valid, jnp.where(late == 1, at, 2 * PAIRS - 1 - at), -1)
        base = []
        for row in entries:
            hit = row[0] == stretch
            for entry in row[1:]:
                hit = jnp.logical_or(hit, entry == stretch)
            base.append(jnp.where(hit, stretch * C, -(1 << 20)))
        key_pos = key_row + jnp.where(lane < C, base[0], base[1])
        seen = (key_pos >= first_pos) & (key_pos <= query_pos)
        bias_ref[pl.ds(slot * HALF, HALF), :] = jnp.where(seen, 0.0, MASKED)

    pltpu.make_async_copy(qdo_ref, qdo_ref, q_sem).wait()
    pltpu.make_async_copy(kv_ref, kv_ref, kv_sem).wait()

    queries = qdo_ref[0].reshape(ROWS, D)
    grads = qdo_ref[1].reshape(ROWS, D)
    keys = kv_ref[:, 0].reshape(SLOTS * HALF, D)
    values = kv_ref[:, 1].reshape(SLOTS * HALF, D)
    last = (((1,), (1,)), ((), ()))
    first = (((0,), (0,)), ((), ()))
    plain = (((1,), (0,)), ((), ()))

    def dot(a, b, dims):
        return lax.dot_general(a, b, dims, preferred_element_type=jnp.float32)

    scores = dot(keys, queries, last) * INV + jnp.concatenate([bias_ref[...]] * PAIR, axis=1)
    top = jnp.max(scores, axis=0, keepdims=True)
    weights = jnp.exp(scores - top)
    mass = jnp.sum(weights, axis=0, keepdims=True)
    grad_weights = dot(values, grads, last)
    inner = jnp.sum(weights * grad_weights, axis=0, keepdims=True)

    stat_ref[b, 0:1] = top
    stat_ref[b, 1:2] = mass
    stat_ref[b, 2:3] = inner
    remote = pltpu.make_async_remote_copy(
        src_ref=stat_ref.at[b], dst_ref=stat_ref.at[b], send_sem=stat_send, recv_sem=stat_sem,
        device_id=(d, mate), device_id_type=MESH,
    )
    remote.start()
    sent.append(remote)
    remote.wait_recv()
    tops = [stat_ref[n, 0:1] for n in range(PAIR)]
    top_all = functools.reduce(jnp.maximum, tops)
    shares = [jnp.exp(t - top_all) for t in tops]
    mass_all = sum(shares[n] * stat_ref[n, 1:2] for n in range(PAIR))
    inner_all = sum(shares[n] * stat_ref[n, 2:3] for n in range(PAIR))
    over = 1.0 / mass_all
    weights = weights * (jnp.exp(top - top_all) * over)
    rounded = weights.astype(jnp.bfloat16)
    grad_scores = (weights * (grad_weights - inner_all * over)).astype(jnp.bfloat16)
    part_ref[:, :, 0] = (dot(grad_scores, queries, plain) * INV).astype(jnp.bfloat16).reshape(SLOTS, 2, QUARTER, D)
    part_ref[:, :, 1] = dot(rounded, grads, plain).astype(jnp.bfloat16).reshape(SLOTS, 2, QUARTER, D)

    def send_back(slot, to, at, may_be_self=False):
        far_plane = pltpu.make_async_remote_copy(
            src_ref=part_ref.at[slot, 1 - p], dst_ref=back_ref.at[p, to], send_sem=back_send, recv_sem=back_sem,
            device_id=(at, across), device_id_type=MESH,
        )
        far_plane.start()
        sent.append(far_plane)
        remote = pltpu.make_async_remote_copy(
            src_ref=part_ref.at[slot, p], dst_ref=back_ref.at[p, to], send_sem=back_send, recv_sem=back_sem,
            device_id=(at, h), device_id_type=MESH,
        )
        if may_be_self:
            local = pltpu.make_async_copy(part_ref.at[slot, p], back_ref.at[p, to], back_sem)
            pl.when(at != d)(remote.start)
            pl.when(at == d)(local.start)
            sent_maybe.append((at, remote))
        else:
            remote.start()
            sent.append(remote)

    for k, at in zip(ODD_STEPS[::-1], odd_with[::-1]):
        send_back(8 - 2 * k, k - 1, at, may_be_self=True)
    for k, at in zip(EVEN_STEPS[::-1], even_from[::-1]):
        send_back(7 - 2 * k, 4 + k, at)
    for n, at in enumerate(far):
        send_back(RECALL + n, 8 + c, at)
    send_back(OTHER, 4, other_core)
    own_across = pltpu.make_async_remote_copy(
        src_ref=part_ref.at[OWN, 1 - p], dst_ref=back_ref.at[p, 10], send_sem=back_send, recv_sem=back_sem,
        device_id=(d, across), device_id_type=MESH,
    )
    own_across.start()
    sent.append(own_across)
    pltpu.make_async_copy(part_ref.at[OWN, p], back_ref.at[p, 10], back_sem).start()

    out = dot(rounded, values, first)
    grad_queries = dot(grad_scores, keys, first) * INV
    rows_ref[:, :, 0] = out.astype(jnp.bfloat16).reshape(PAIR, 2, C, D)
    rows_ref[:, :, 1] = grad_queries.astype(jnp.bfloat16).reshape(PAIR, 2, C, D)
    pltpu.make_async_copy(rows_ref.at[b, 0], got_ref.at[b, 0], rows_sem).start()
    for of, which, to in ((1 - b, 0, (d, mate)), (1 - b, 1, (other_core, mate)), (b, 1, (other_core, h))):
        remote = pltpu.make_async_remote_copy(
            src_ref=rows_ref.at[of, which], dst_ref=got_ref.at[b, which], send_sem=rows_send, recv_sem=rows_sem,
            device_id=to, device_id_type=MESH,
        )
        remote.start()
        sent.append(remote)

    pltpu.make_async_copy(back_ref, back_ref, back_sem).wait()

    def read(n):
        return back_ref[0, n].astype(jnp.float32) + back_ref[1, n].astype(jnp.float32)

    recalled = read(8) + read(9)
    to_even = jnp.where(late == c, 1.0, 0.0)
    even_total = read(10) + read(5) + read(6) + read(7) + recalled * to_even
    odd_total = read(4) + read(0) + read(1) + read(2) + read(3) + recalled * (1.0 - to_even)
    sums_out[h, c] = even_total.astype(jnp.bfloat16)
    sums_out[h, 1 - c] = odd_total.astype(jnp.bfloat16)
    sum_sends = [
        pltpu.make_async_remote_copy(
            src_ref=sums_out.at[h], dst_ref=sums_out.at[h], send_sem=sums_send.at[k], recv_sem=sums_sem.at[k],
            device_id=(d, at), device_id_type=MESH,
        )
        for k, at in enumerate(heads)
    ]
    for copy in sum_sends:
        copy.start()

    pltpu.make_async_copy(got_ref, got_ref, rows_sem).wait()
    for which, place in ((0, c), (1, 1 - c)):
        total = sum(got_ref[n, which].astype(jnp.float32) for n in range(PAIR))
        for n in range(2):
            rows_out[n, place] = total[n].astype(jnp.bfloat16)

    for copy in sent:
        copy.wait_send()
    for at, copy in sent_maybe:
        pl.when(at != d)(copy.wait_send)
    for copy in sum_sends:
        copy.wait_send()
        copy.wait_recv()


def lay_out_kernel(rows_ref, sums_ref, out_ref, dq_ref, dk_ref, dv_ref):
    out_ref[...] = rows_ref[0].reshape(2 * C, D)
    dq_ref[...] = rows_ref[1].reshape(2 * C, D)
    for h in range(HEADS):
        g, q = h // GROUP, 2 * (h % PAIR) + h // PAIR % 2
        for s in range(2):
            rows = slice(s * C + q * QUARTER, s * C + (q + 1) * QUARTER)
            dk_ref[g, rows] = sums_ref[h, s, 0]
            dv_ref[g, rows] = sums_ref[h, s, 1]


def on_device(queries, keys, values, grad_out, episode_lengths, key_stretches):
    vmem = pl.BlockSpec(memory_space=pltpu.VMEM)
    dma = pltpu.SemaphoreType.DMA
    bf16 = jnp.bfloat16
    inputs = [
        pltpu.with_memory_space_constraint(x, pltpu.HBM)
        for x in (queries, keys, values, grad_out, episode_lengths, key_stretches.T)
    ]
    rows, sums = pl.pallas_call(
        attend_kernel,
        out_shape=(
            pltpu.VMEM((2, 2, C, D), bf16),
            pltpu.VMEM((HEADS, 2, 2, QUARTER, D), bf16),
        ),
        in_specs=[pl.BlockSpec(memory_space=pltpu.HBM)] * 6,
        out_specs=(vmem, vmem),
        scratch_shapes=[
            pltpu.VMEM((2, PAIR, 2, C, D), bf16),
            pltpu.VMEM((SLOTS, 2, HALF, D), bf16),
            pltpu.VMEM((SLOTS * HALF, 2 * C), jnp.float32),
            pltpu.VMEM((PAIR, 8, ROWS), jnp.float32),
            pltpu.VMEM((SLOTS, 2, 2, QUARTER, D), bf16),
            pltpu.VMEM((2, SLOTS, 2, QUARTER, D), bf16),
            pltpu.VMEM((PAIR, 2, 2, C, D), bf16),
            pltpu.VMEM((PAIR, 2, 2, C, D), bf16),
            pltpu.SMEM((HEADS,), jnp.int32),
            pltpu.SMEM((4, 2 * PAIRS), jnp.int32),
            dma((2,)), dma, dma, dma, dma, dma, dma((HEADS - 1,)),
            dma, dma, dma, dma, dma, dma((HEADS - 1,)),
        ],
        compiler_params=pltpu.CompilerParams(
            collective_id=0, has_side_effects=True, vmem_limit_bytes=16 * 1024 * 1024
        ),
        name="attend",
    )(*inputs)
    half = jax.ShapeDtypeStruct((2 * C, D), bf16)
    both = jax.ShapeDtypeStruct((2, 2 * C, D), bf16)
    return pl.pallas_call(
        lay_out_kernel,
        out_shape=(half, half, both, both),
        in_specs=[vmem] * 2,
        out_specs=(vmem,) * 4,
        name="lay_out",
    )(*(pltpu.with_memory_space_constraint(x, pltpu.VMEM) for x in (rows, sums)))


def solution(mesh):
    return jax.shard_map(
        on_device,
        mesh=mesh,
        in_specs=(
            P("ctx", "head"),
            P(None, "ctx", None),
            P(None, "ctx", None),
            P("ctx", "head"),
            P(),
            P(),
        ),
        out_specs=(P("ctx", "head"), P("ctx", "head"), P(None, "ctx", None), P(None, "ctx", None)),
        check_vma=False,
    )
```

time: 40.9 us -> 37 us (0.905)
  the two profiles are of different devices: /device:TPU:23 before, /device:TPU:1 now
where the time goes in v2:
time: 37 us; the launch traced here: 36.9 us
  Pallas kernels  36.2 us (98%)
  between operations  0.64 us (2%)
    pallas_call x1, Pallas kernels, on_device(): pl.pallas_call(attend_kernel, out_shape=(pltpu.VMEM((2, 2, C, D), bf16),...  35.5 us

profile of v2, /device:TPU:1, one launch (start us, length us, event | category | flops | bytes accessed | tf_op | source)
XLA Modules:
  0.0 36.9 jit_solution(13644097231325473149)
XLA Ops:
  0.6 35.5 %attend.1 = (bf16[2,2,64,128]{3,2,1,0:T(8,128)(2,1)S(1)}, bf16[8,2,2,16,128]{4,3,2,1,0:T(8,128)(2,1)S(1)}) custom-call(bf16[128,128]{1,0:T(8,128)(2,1)} %q_hbm.1, bf16[2,128,128]{2,1,0:T(8,128)(2,1)} %k_hbm.1, bf16[2,128,128]{2,1,0:T(8,128)(2,1)} %v_hbm.1, bf16[128,128]{1,0:T(8,128)(2,1)} %do_hbm.1, s32[8]{0:T(128)} %ep_hbm.1, s32[4,128]{1,0:T(4,128)} %bitcast.1), custom_call_target="tpu_custom_call" | custom-call | tf_op jit(solution)/shard_map/attend/pallas_call | solution.py:306
  36.2 0.7 %lay_out.1 = (bf16[128,128]{1,0:T(8,128)(2,1)}, bf16[128,128]{1,0:T(8,128)(2,1)}, bf16[2,128,128]{2,1,0:T(8,128)(2,1)}, bf16[2,128,128]{2,1,0:T(8,128)(2,1)}) custom-call(bf16[2,2,64,128]{3,2,1,0:T(8,128)(2,1)S(1)} %get-tuple-element.6.rows_ref, bf16[8,2,2,16,128]{4,3,2,1,0:T(8,128)(2,1)S(1)} %get-tuple-element.7.sums_ref), custom_call_target="tpu_custom_call" | custom-call | tf_op jit(solution)/shard_map/lay_out/pallas_call | solution.py:335

commit v3 on v2

--- a/solution.py
+++ b/solution.py
@@ -18,6 +18,7 @@
 PAIRS = 64
 ROWS = PAIR * 2 * C
 CHIPS = 32
+Z_CHIPS = 8
 SLOTS = 11
 OWN, OTHER, RECALL = 7, 8, 9
 D = 128
@@ -35,17 +36,18 @@
 def attend_kernel(
     q_hbm, k_hbm, v_hbm, do_hbm, ep_hbm, ks_hbm,
     rows_out, sums_out,
-    qdo_ref, kv_ref, bias_ref, stat_ref, part_ref, back_ref, rows_ref, got_ref,
+    qdo_ref, kv_ref, bias_ref, stat_ref, part_ref, even_ref, odd_ref, recall_ref, acc_ref, rows_ref, got_ref,
     ep_ref, ks_ref,
-    in_sems, kv_sem, q_sem, stat_sem, back_sem, rows_sem, sums_sem,
+    in_sems, kv_sem, q_sem, stat_sem, even_sem, odd_sem, recall_sem, rows_sem, sums_sem,
     kv_send, q_send, stat_send, back_send, rows_send, sums_send,
 ):
     d = lax.axis_index("ctx")
     h = lax.axis_index("head")
     m, c = d // 2, d % 2
-    g, p, b = h // GROUP, h // PAIR % 2, h % PAIR
-    mate = h + 1 - 2 * b
-    across = h + 2 - 4 * p
+    g, p, b = h // GROUP, h % PAIR, h // PAIR % 2
+    mate = h + 2 - 4 * b
+    across = h + 1 - 2 * p
+    opposite = h + 4 - 8 * g
     mine = jnp.where(c == 0, m, PAIRS - 1 - m)
     other = PAIRS - 1 - mine
     other_core = 2 * m + 1 - c
@@ -65,11 +67,9 @@
 
     for at in odd_with[::-1]:
         pl.when(at != d)(functools.partial(greet, at, h))
-        greet(at, across)
-    for at in even_to + even_from + far + [other_core]:
+    for at in even_from[::-1] + far + [other_core]:
         greet(at, h)
-        greet(at, across)
-    for at in heads:
+    for at in (mate, across, opposite):
         greet(d, at)
     greet(other_core, mate)
 
@@ -88,7 +88,7 @@
         copy.start()
 
     self_count = jnp.where(lax.rem(mine, PAIRS // 2) < 2, 1, 0)
-    pl.semaphore_wait(barrier, 2 * (6 + 4 + 1 + 2) + 7 + 1 - self_count)
+    pl.semaphore_wait(barrier, 4 + 3 + 2 + 1 + 3 + 1 - self_count)
 
     sent, sent_maybe = [], []
 
@@ -119,13 +119,13 @@
 
     for k, at in zip(ODD_STEPS[::-1], odd_with[::-1]):
         send_kv(1 - c, 8 - 2 * k, at, may_be_self=True)
-    send_q(even_rows, 0, (d, mate))
-    send_q(odd_rows, 1, (other_core, mate))
     for k, at in zip(EVEN_STEPS[::-1], even_to[::-1]):
         send_kv(c, 7 - 2 * k, at)
     for at in far:
         send_kv(late, RECALL + c, at)
     send_kv(1 - c, OTHER, other_core)
+    send_q(even_rows, 0, (d, mate))
+    send_q(odd_rows, 1, (other_core, mate))
     send_q(odd_rows, 1, (other_core, h))
 
     for copy in loads:
@@ -200,19 +200,19 @@
     part_ref[:, :, 0] = (dot(grad_scores, queries, plain) * INV).astype(jnp.bfloat16).reshape(SLOTS, 2, QUARTER, D)
     part_ref[:, :, 1] = dot(rounded, grads, plain).astype(jnp.bfloat16).reshape(SLOTS, 2, QUARTER, D)
 
-    def send_back(slot, to, at, may_be_self=False):
+    def send_back(slot, buffer, sem, to, at, may_be_self=False):
         far_plane = pltpu.make_async_remote_copy(
-            src_ref=part_ref.at[slot, 1 - p], dst_ref=back_ref.at[p, to], send_sem=back_send, recv_sem=back_sem,
+            src_ref=part_ref.at[slot, 1 - p], dst_ref=buffer.at[p, to], send_sem=back_send, recv_sem=sem,
             device_id=(at, across), device_id_type=MESH,
         )
         far_plane.start()
         sent.append(far_plane)
         remote = pltpu.make_async_remote_copy(
-            src_ref=part_ref.at[slot, p], dst_ref=back_ref.at[p, to], send_sem=back_send, recv_sem=back_sem,
+            src_ref=part_ref.at[slot, p], dst_ref=buffer.at[p, to], send_sem=back_send, recv_sem=sem,
             device_id=(at, h), device_id_type=MESH,
         )
         if may_be_self:
-            local = pltpu.make_async_copy(part_ref.at[slot, p], back_ref.at[p, to], back_sem)
+            local = pltpu.make_async_copy(part_ref.at[slot, p], buffer.at[p, to], sem)
             pl.when(at != d)(remote.start)
             pl.when(at == d)(local.start)
             sent_maybe.append((at, remote))
@@ -221,19 +221,19 @@
             sent.append(remote)
 
     for k, at in zip(ODD_STEPS[::-1], odd_with[::-1]):
-        send_back(8 - 2 * k, k - 1, at, may_be_self=True)
+        send_back(8 - 2 * k, odd_ref, odd_sem, k - 1, at, may_be_self=True)
     for k, at in zip(EVEN_STEPS[::-1], even_from[::-1]):
-        send_back(7 - 2 * k, 4 + k, at)
+        send_back(7 - 2 * k, even_ref, even_sem, k - 1, at)
     for n, at in enumerate(far):
-        send_back(RECALL + n, 8 + c, at)
-    send_back(OTHER, 4, other_core)
+        send_back(RECALL + n, recall_ref, recall_sem, c, at)
+    send_back(OTHER, odd_ref, odd_sem, 4, other_core)
     own_across = pltpu.make_async_remote_copy(
-        src_ref=part_ref.at[OWN, 1 - p], dst_ref=back_ref.at[p, 10], send_sem=back_send, recv_sem=back_sem,
+        src_ref=part_ref.at[OWN, 1 - p], dst_ref=even_ref.at[p, 3], send_sem=back_send, recv_sem=even_sem,
         device_id=(d, across), device_id_type=MESH,
     )
     own_across.start()
     sent.append(own_across)
-    pltpu.make_async_copy(part_ref.at[OWN, p], back_ref.at[p, 10], back_sem).start()
+    pltpu.make_async_copy(part_ref.at[OWN, p], even_ref.at[p, 3], even_sem).start()
 
     out = dot(rounded, values, first)
     grad_queries = dot(grad_scores, keys, first) * INV
@@ -248,26 +248,27 @@
         remote.start()
         sent.append(remote)
 
-    pltpu.make_async_copy(back_ref, back_ref, back_sem).wait()
-
-    def read(n):
-        return back_ref[0, n].astype(jnp.float32) + back_ref[1, n].astype(jnp.float32)
-
-    recalled = read(8) + read(9)
-    to_even = jnp.where(late == c, 1.0, 0.0)
-    even_total = read(10) + read(5) + read(6) + read(7) + recalled * to_even
-    odd_total = read(4) + read(0) + read(1) + read(2) + read(3) + recalled * (1.0 - to_even)
-    sums_out[h, c] = even_total.astype(jnp.bfloat16)
-    sums_out[h, 1 - c] = odd_total.astype(jnp.bfloat16)
-    sum_sends = [
-        pltpu.make_async_remote_copy(
-            src_ref=sums_out.at[h], dst_ref=sums_out.at[h], send_sem=sums_send.at[k], recv_sem=sums_sem.at[k],
-            device_id=(d, at), device_id_type=MESH,
-        )
-        for k, at in enumerate(heads)
-    ]
-    for copy in sum_sends:
-        copy.start()
+    sum_sends = []
+
+    def add_up(buffer, sem, start):
+        pltpu.make_async_copy(buffer, buffer, sem).wait()
+        total = jnp.sum(buffer[...].astype(jnp.float32), axis=(0, 1))
+        acc_ref[...] = total if start else acc_ref[...] + total
+
+    first_place = lax.rem(m, Z_CHIPS) // (Z_CHIPS // 2)
+    for turn, place in enumerate((first_place, 1 - first_place)):
+        pl.when(place == c)(functools.partial(add_up, even_ref, even_sem, True))
+        pl.when(place != c)(functools.partial(add_up, odd_ref, odd_sem, True))
+        pl.when(place == late)(functools.partial(add_up, recall_ref, recall_sem, False))
+        sums_out[h, place] = acc_ref[...].astype(jnp.bfloat16)
+        for k, at in enumerate(heads):
+            remote = pltpu.make_async_remote_copy(
+                src_ref=sums_out.at[h, place], dst_ref=sums_out.at[h, place],
+                send_sem=sums_send.at[turn, k], recv_sem=sums_sem.at[turn, k],
+                device_id=(d, at), device_id_type=MESH,
+            )
+            remote.start()
+            sum_sends.append(remote)
 
     pltpu.make_async_copy(got_ref, got_ref, rows_sem).wait()
     for which, place in ((0, c), (1, 1 - c)):
@@ -288,7 +289,7 @@
     out_ref[...] = rows_ref[0].reshape(2 * C, D)
     dq_ref[...] = rows_ref[1].reshape(2 * C, D)
     for h in range(HEADS):
-        g, q = h // GROUP, 2 * (h % PAIR) + h // PAIR % 2
+        g, q = divmod(h, GROUP)
         for s in range(2):
             rows = slice(s * C + q * QUARTER, s * C + (q + 1) * QUARTER)
             dk_ref[g, rows] = sums_ref[h, s, 0]
@@ -317,13 +318,16 @@
             pltpu.VMEM((SLOTS * HALF, 2 * C), jnp.float32),
             pltpu.VMEM((PAIR, 8, ROWS), jnp.float32),
             pltpu.VMEM((SLOTS, 2, 2, QUARTER, D), bf16),
-            pltpu.VMEM((2, SLOTS, 2, QUARTER, D), bf16),
+            pltpu.VMEM((2, 4, 2, QUARTER, D), bf16),
+            pltpu.VMEM((2, 5, 2, QUARTER, D), bf16),
+            pltpu.VMEM((2, 2, 2, QUARTER, D), bf16),
+            pltpu.VMEM((2, QUARTER, D), jnp.float32),
             pltpu.VMEM((PAIR, 2, 2, C, D), bf16),
             pltpu.VMEM((PAIR, 2, 2, C, D), bf16),
             pltpu.SMEM((HEADS,), jnp.int32),
             pltpu.SMEM((4, 2 * PAIRS), jnp.int32),
-            dma((2,)), dma, dma, dma, dma, dma, dma((HEADS - 1,)),
-            dma, dma, dma, dma, dma, dma((HEADS - 1,)),
+            dma((2,)), dma, dma, dma, dma, dma, dma, dma, dma((2, HEADS - 1)),
+            dma, dma, dma, dma, dma, dma((2, HEADS - 1)),
         ],
         compiler_params=pltpu.CompilerParams(
             collective_id=0, has_side_effects=True, vmem_limit_bytes=16 * 1024 * 1024

time: 37 us -> 36.9 us (level)
  no operation moved by 1% of the time
where the time goes in v3:
time: 36.9 us; the launch traced here: 36.7 us
  Pallas kernels  36.1 us (98%)
  between operations  0.64 us (2%)
    pallas_call x1, Pallas kernels, on_device(): pl.pallas_call(attend_kernel, out_shape=(pltpu.VMEM((2, 2, C, D), bf16),...  35.4 us

profile of v3, /device:TPU:1, one launch (start us, length us, event | category | flops | bytes accessed | tf_op | source)
XLA Modules:
  0.0 36.7 jit_solution(16479960961598780470)
XLA Ops:
  0.6 35.4 %attend.1 = (bf16[2,2,64,128]{3,2,1,0:T(8,128)(2,1)S(1)}, bf16[8,2,2,16,128]{4,3,2,1,0:T(8,128)(2,1)S(1)}) custom-call(bf16[128,128]{1,0:T(8,128)(2,1)} %q_hbm.1, bf16[2,128,128]{2,1,0:T(8,128)(2,1)} %k_hbm.1, bf16[2,128,128]{2,1,0:T(8,128)(2,1)} %v_hbm.1, bf16[128,128]{1,0:T(8,128)(2,1)} %do_hbm.1, s32[8]{0:T(128)} %ep_hbm.1, s32[4,128]{1,0:T(4,128)} %bitcast.1), custom_call_target="tpu_custom_call" | custom-call | tf_op jit(solution)/shard_map/attend/pallas_call | solution.py:307
  36.0 0.7 %lay_out.1 = (bf16[128,128]{1,0:T(8,128)(2,1)}, bf16[128,128]{1,0:T(8,128)(2,1)}, bf16[2,128,128]{2,1,0:T(8,128)(2,1)}, bf16[2,128,128]{2,1,0:T(8,128)(2,1)}) custom-call(bf16[2,2,64,128]{3,2,1,0:T(8,128)(2,1)S(1)} %get-tuple-element.6.rows_ref, bf16[8,2,2,16,128]{4,3,2,1,0:T(8,128)(2,1)S(1)} %get-tuple-element.7.sums_ref), custom_call_target="tpu_custom_call" | custom-call | tf_op jit(solution)/shard_map/lay_out/pallas_call | solution.py:339

commit v4 on v3

--- a/solution.py
+++ b/solution.py
@@ -39,7 +39,7 @@
     qdo_ref, kv_ref, bias_ref, stat_ref, part_ref, even_ref, odd_ref, recall_ref, acc_ref, rows_ref, got_ref,
     ep_ref, ks_ref,
     in_sems, kv_sem, q_sem, stat_sem, even_sem, odd_sem, recall_sem, rows_sem, sums_sem,
-    kv_send, q_send, stat_send, back_send, rows_send, sums_send,
+    kv_send, q_send, stat_send, back_send, rows_send, sums_send, opposite_sem,
 ):
     d = lax.axis_index("ctx")
     h = lax.axis_index("head")
@@ -69,8 +69,9 @@
         pl.when(at != d)(functools.partial(greet, at, h))
     for at in even_from[::-1] + far + [other_core]:
         greet(at, h)
-    for at in (mate, across, opposite):
+    for at in (mate, across):
         greet(d, at)
+    pl.when(g == 0)(functools.partial(greet, d, opposite))
     greet(other_core, mate)
 
     even_rows, odd_rows = pl.ds(c * C, C), pl.ds((1 - c) * C, C)
@@ -88,7 +89,7 @@
         copy.start()
 
     self_count = jnp.where(lax.rem(mine, PAIRS // 2) < 2, 1, 0)
-    pl.semaphore_wait(barrier, 4 + 3 + 2 + 1 + 3 + 1 - self_count)
+    pl.semaphore_wait(barrier, 4 + 3 + 2 + 1 + 2 + 1 + g - self_count)
 
     sent, sent_maybe = [], []
 
@@ -188,6 +189,10 @@
     remote.start()
     sent.append(remote)
     remote.wait_recv()
+    @pl.when(g == 1)
+    def _():
+        pl.semaphore_signal(opposite_sem, inc=1, device_id=(d, opposite), device_id_type=MESH)
+
     tops = [stat_ref[n, 0:1] for n in range(PAIR)]
     top_all = functools.reduce(jnp.maximum, tops)
     shares = [jnp.exp(t - top_all) for t in tops]
@@ -255,8 +260,8 @@
         total = jnp.sum(buffer[...].astype(jnp.float32), axis=(0, 1))
         acc_ref[...] = total if start else acc_ref[...] + total
 
-    first_place = lax.rem(m, Z_CHIPS) // (Z_CHIPS // 2)
-    for turn, place in enumerate((first_place, 1 - first_place)):
+    pl.when(g == 0)(lambda: pl.semaphore_wait(opposite_sem, 1))
+    for turn, place in enumerate((1, 0)):
         pl.when(place == c)(functools.partial(add_up, even_ref, even_sem, True))
         pl.when(place != c)(functools.partial(add_up, odd_ref, odd_sem, True))
         pl.when(place == late)(functools.partial(add_up, recall_ref, recall_sem, False))
@@ -327,7 +332,7 @@
             pltpu.SMEM((HEADS,), jnp.int32),
             pltpu.SMEM((4, 2 * PAIRS), jnp.int32),
             dma((2,)), dma, dma, dma, dma, dma, dma, dma, dma((2, HEADS - 1)),
-            dma, dma, dma, dma, dma, dma((2, HEADS - 1)),
+            dma, dma, dma, dma, dma, dma((2, HEADS - 1)), pltpu.SemaphoreType.REGULAR,
         ],
         compiler_params=pltpu.CompilerParams(
             collective_id=0, has_side_effects=True, vmem_limit_bytes=16 * 1024 * 1024

time: 36.9 us -> 35.6 us (0.965)
  Pallas kernels: 36.1 us -> 34.7 us
    pallas_call x1, Pallas kernels: 35.4 us -> 34 us  [on_device(): pl.pallas_call(attend_kernel, out_shape=(pltpu.VMEM((2, 2, C, D), bf16),...]
where the time goes in v4:
time: 35.6 us; the launch traced here: 35.4 us
  Pallas kernels  34.7 us (97%)
  between operations  0.64 us (2%)
    pallas_call x1, Pallas kernels, on_device(): pl.pallas_call(attend_kernel, out_shape=(pltpu.VMEM((2, 2, C, D), bf16),...  34 us

profile of v4, /device:TPU:1, one launch (start us, length us, event | category | flops | bytes accessed | tf_op | source)
XLA Modules:
  0.0 35.4 jit_solution(17117650328025271877)
XLA Ops:
  0.6 34.0 %attend.1 = (bf16[2,2,64,128]{3,2,1,0:T(8,128)(2,1)S(1)}, bf16[8,2,2,16,128]{4,3,2,1,0:T(8,128)(2,1)S(1)}) custom-call(bf16[128,128]{1,0:T(8,128)(2,1)} %q_hbm.1, bf16[2,128,128]{2,1,0:T(8,128)(2,1)} %k_hbm.1, bf16[2,128,128]{2,1,0:T(8,128)(2,1)} %v_hbm.1, bf16[128,128]{1,0:T(8,128)(2,1)} %do_hbm.1, s32[8]{0:T(128)} %ep_hbm.1, s32[4,128]{1,0:T(4,128)} %bitcast.1), custom_call_target="tpu_custom_call" | custom-call | tf_op jit(solution)/shard_map/attend/pallas_call | solution.py:312
  34.7 0.7 %lay_out.1 = (bf16[128,128]{1,0:T(8,128)(2,1)}, bf16[128,128]{1,0:T(8,128)(2,1)}, bf16[2,128,128]{2,1,0:T(8,128)(2,1)}, bf16[2,128,128]{2,1,0:T(8,128)(2,1)}) custom-call(bf16[2,2,64,128]{3,2,1,0:T(8,128)(2,1)S(1)} %get-tuple-element.6.rows_ref, bf16[8,2,2,16,128]{4,3,2,1,0:T(8,128)(2,1)S(1)} %get-tuple-element.7.sums_ref), custom_call_target="tpu_custom_call" | custom-call | tf_op jit(solution)/shard_map/lay_out/pallas_call | solution.py:344

commit v5 on v4

--- a/solution.py
+++ b/solution.py
@@ -58,7 +58,7 @@
     even_from = [device_of(mine - k) for k in EVEN_STEPS]
     odd_with = [device_of(other + k) for k in ODD_STEPS]
     far = [2 * far_chip, 2 * far_chip + 1]
-    heads = [(h + k) % HEADS for k in (4, 3, 5, 2, 6, 1, 7)]
+    heads = [(1 - g) * GROUP + (h + k) % GROUP for k in (0, 1, 3, 2)] + [g * GROUP + (h + k) % GROUP for k in (2, 1, 3)]
 
     barrier = pltpu.get_barrier_semaphore()
 

time: 35.6 us -> 35.3 us (level)
  Pallas kernels: 34.7 us -> 34.2 us
    pallas_call x1, Pallas kernels: 34 us -> 33.5 us  [on_device(): pl.pallas_call(attend_kernel, out_shape=(pltpu.VMEM((2, 2, C, D), bf16),...]
where the time goes in v5:
time: 35.3 us; the launch traced here: 34.8 us
  Pallas kernels  34.2 us (97%)
  between operations  0.64 us (2%)
    pallas_call x1, Pallas kernels, on_device(): pl.pallas_call(attend_kernel, out_shape=(pltpu.VMEM((2, 2, C, D), bf16),...  33.5 us

profile of v5, /device:TPU:1, one launch (start us, length us, event | category | flops | bytes accessed | tf_op | source)
XLA Modules:
  0.0 34.8 jit_solution(9523393658641724123)
XLA Ops:
  0.6 33.5 %attend.1 = (bf16[2,2,64,128]{3,2,1,0:T(8,128)(2,1)S(1)}, bf16[8,2,2,16,128]{4,3,2,1,0:T(8,128)(2,1)S(1)}) custom-call(bf16[128,128]{1,0:T(8,128)(2,1)} %q_hbm.1, bf16[2,128,128]{2,1,0:T(8,128)(2,1)} %k_hbm.1, bf16[2,128,128]{2,1,0:T(8,128)(2,1)} %v_hbm.1, bf16[128,128]{1,0:T(8,128)(2,1)} %do_hbm.1, s32[8]{0:T(128)} %ep_hbm.1, s32[4,128]{1,0:T(4,128)} %bitcast.1), custom_call_target="tpu_custom_call" | custom-call | tf_op jit(solution)/shard_map/attend/pallas_call | solution.py:312
  34.1 0.7 %lay_out.1 = (bf16[128,128]{1,0:T(8,128)(2,1)}, bf16[128,128]{1,0:T(8,128)(2,1)}, bf16[2,128,128]{2,1,0:T(8,128)(2,1)}, bf16[2,128,128]{2,1,0:T(8,128)(2,1)}) custom-call(bf16[2,2,64,128]{3,2,1,0:T(8,128)(2,1)S(1)} %get-tuple-element.6.rows_ref, bf16[8,2,2,16,128]{4,3,2,1,0:T(8,128)(2,1)S(1)} %get-tuple-element.7.sums_ref), custom_call_target="tpu_custom_call" | custom-call | tf_op jit(solution)/shard_map/lay_out/pallas_call | solution.py:344

commit v6 on v5

--- a/solution.py
+++ b/solution.py
@@ -225,12 +225,12 @@
             remote.start()
             sent.append(remote)
 
+    for n, at in enumerate(far):
+        send_back(RECALL + n, recall_ref, recall_sem, c, at)
     for k, at in zip(ODD_STEPS[::-1], odd_with[::-1]):
         send_back(8 - 2 * k, odd_ref, odd_sem, k - 1, at, may_be_self=True)
     for k, at in zip(EVEN_STEPS[::-1], even_from[::-1]):
         send_back(7 - 2 * k, even_ref, even_sem, k - 1, at)
-    for n, at in enumerate(far):
-        send_back(RECALL + n, recall_ref, recall_sem, c, at)
     send_back(OTHER, odd_ref, odd_sem, 4, other_core)
     own_across = pltpu.make_async_remote_copy(
         src_ref=part_ref.at[OWN, 1 - p], dst_ref=even_ref.at[p, 3], send_sem=back_send, recv_sem=even_sem,

time: 35.3 us -> 35.5 us (level)
  Pallas kernels: 34.2 us -> 34.7 us
    pallas_call x1, Pallas kernels: 33.5 us -> 34 us  [on_device(): pl.pallas_call(attend_kernel, out_shape=(pltpu.VMEM((2, 2, C, D), bf16),...]
where the time goes in v6:
time: 35.5 us; the launch traced here: 35.3 us
  Pallas kernels  34.7 us (98%)
  between operations  0.64 us (2%)
    pallas_call x1, Pallas kernels, on_device(): pl.pallas_call(attend_kernel, out_shape=(pltpu.VMEM((2, 2, C, D), bf16),...  34 us

profile of v6, /device:TPU:1, one launch (start us, length us, event | category | flops | bytes accessed | tf_op | source)
XLA Modules:
  0.0 35.3 jit_solution(126738758671346330)
XLA Ops:
  0.6 34.0 %attend.1 = (bf16[2,2,64,128]{3,2,1,0:T(8,128)(2,1)S(1)}, bf16[8,2,2,16,128]{4,3,2,1,0:T(8,128)(2,1)S(1)}) custom-call(bf16[128,128]{1,0:T(8,128)(2,1)} %q_hbm.1, bf16[2,128,128]{2,1,0:T(8,128)(2,1)} %k_hbm.1, bf16[2,128,128]{2,1,0:T(8,128)(2,1)} %v_hbm.1, bf16[128,128]{1,0:T(8,128)(2,1)} %do_hbm.1, s32[8]{0:T(128)} %ep_hbm.1, s32[4,128]{1,0:T(4,128)} %bitcast.1), custom_call_target="tpu_custom_call" | custom-call | tf_op jit(solution)/shard_map/attend/pallas_call | solution.py:312
  34.6 0.7 %lay_out.1 = (bf16[128,128]{1,0:T(8,128)(2,1)}, bf16[128,128]{1,0:T(8,128)(2,1)}, bf16[2,128,128]{2,1,0:T(8,128)(2,1)}, bf16[2,128,128]{2,1,0:T(8,128)(2,1)}) custom-call(bf16[2,2,64,128]{3,2,1,0:T(8,128)(2,1)S(1)} %get-tuple-element.6.rows_ref, bf16[8,2,2,16,128]{4,3,2,1,0:T(8,128)(2,1)S(1)} %get-tuple-element.7.sums_ref), custom_call_target="tpu_custom_call" | custom-call | tf_op jit(solution)/shard_map/lay_out/pallas_call | solution.py:344
